TPU v7x, 32 devices: a whole 2x2x4 slice. The times are simulated.
32 devices in a mesh: wide: 8 (over y, x, core), narrow: 4 (over z).
Axes of the slice: x: 2, y: 2, z: 4, core: 2. Of those that a mesh axis runs over, the one named last changes fastest.
Arguments:
- tokens: bfloat16 [4096, 2048], P(('wide', 'narrow')), may hold values from -6 to 6
- cotangent: bfloat16 [4096, 2048], P(('wide', 'narrow')), may hold values from -1.5 to 1.5
- gate_prob: float32 [4096], P(('wide', 'narrow')), may hold values from 0.2 to 1
- expert_ids: int32 [4096, 1], P(('wide', 'narrow')), may hold values from 0 to 31; in each aligned block of 128 rows (0 to 127, 128 to 255, ...) at most 6 rows name the same one
- keep_mask: int32 [4096], P(('wide', 'narrow')), may hold values 0 or 1
- w_gate: bfloat16 [32, 2048, 704], P(('wide', 'narrow')), may hold values from -0.125 to 0.125
- w_up: bfloat16 [32, 2048, 704], P(('wide', 'narrow')), may hold values from -0.125 to 0.125
- w_down: bfloat16 [32, 704, 2048], P(('wide', 'narrow')), may hold values from -0.21875 to 0.21875
Outputs:
- grad_tokens: bfloat16 [4096, 2048], P(('wide', 'narrow'))
- grad_prob: float32 [4096], P(('wide', 'narrow'))
- grad_gate: bfloat16 [32, 2048, 704], P(('wide', 'narrow'))
- grad_up: bfloat16 [32, 2048, 704], P(('wide', 'narrow'))
- grad_down: bfloat16 [32, 704, 2048], P(('wide', 'narrow'))
Inputs may be any that keep to these rules, and one draw needn't show every extreme that they name: `expert_ids`: among the 128 rows of one device no expert is named more than 6 times; in every draw some device names some expert exactly 6 times.
All inputs are finite; a program needn't handle non-finite values. No bound on the sum of `keep_mask` on one device may be relied on, other than what follows from the above.
Results may differ from a plain program's by a relative error of at most 0.015.
Values may be sent and summed in bfloat16 or wider, within the bound.
A program may use at most 64 MiB of HBM per device.

v0:
```python
import jax
import jax.numpy as jnp
from jax import lax
from jax.sharding import PartitionSpec as P


def expert_grad(rows_in, rows_cot, rows_prob, wgate, wup, wdown):
    g = jnp.dot(rows_in, wgate, preferred_element_type=jnp.float32)
    u = jnp.dot(rows_in, wup, preferred_element_type=jnp.float32)
    sig = jax.nn.sigmoid(g)
    silu_g = g * sig
    hidden = (silu_g * u).astype(jnp.bfloat16)
    out_rows = jnp.dot(hidden, wdown, preferred_element_type=jnp.float32)
    prob_grad = jnp.sum(rows_cot.astype(jnp.float32) * out_rows, axis=1)
    dout = (rows_prob[:, None] * rows_cot.astype(jnp.float32)).astype(jnp.bfloat16)
    gdown = lax.dot_general(
        hidden, dout, (((0,), (0,)), ((), ())), preferred_element_type=jnp.float32
    ).astype(jnp.bfloat16)
    dhid = lax.dot_general(
        dout, wdown, (((1,), (1,)), ((), ())), preferred_element_type=jnp.float32
    )
    dgate = (dhid * u * sig * (1.0 + g * (1.0 - sig))).astype(jnp.bfloat16)
    dup = (dhid * silu_g).astype(jnp.bfloat16)
    ggate = lax.dot_general(
        rows_in, dgate, (((0,), (0,)), ((), ())), preferred_element_type=jnp.float32
    ).astype(jnp.bfloat16)
    gup = lax.dot_general(
        rows_in, dup, (((0,), (0,)), ((), ())), preferred_element_type=jnp.float32
    ).astype(jnp.bfloat16)
    dx_rows = lax.dot_general(
        dgate, wgate, (((1,), (1,)), ((), ())), preferred_element_type=jnp.float32
    )
    dx_rows = dx_rows + lax.dot_general(
        dup, wup, (((1,), (1,)), ((), ())), preferred_element_type=jnp.float32
    )
    return (dx_rows.astype(jnp.bfloat16), prob_grad, ggate, gup, gdown)


def on_device(tokens, cotangent, gate_prob, expert_ids, keep_mask, w_gate, w_up, w_down):
    tok_rows = tokens.shape[0]
    width = tokens.shape[1]
    n_wide = lax.axis_size("wide")
    n_narrow = lax.axis_size("narrow")
    sources = n_wide * n_narrow
    experts = sources * w_gate.shape[0]
    capacity = max(2, 5 * tok_rows // (4 * experts) + 1)
    ids = expert_ids[:, 0]
    kept = keep_mask == 1
    order = jnp.arange(tok_rows, dtype=jnp.int32)
    earlier = (ids[:, None] == ids[None, :]) & kept[None, :] & (order[None, :] < order[:, None])
    slot = jnp.sum(earlier.astype(jnp.int32), axis=1)
    target = jnp.where(kept, ids * capacity + slot, -1)
    places = jnp.arange(experts * capacity, dtype=jnp.int32)
    route = places[:, None] == target[None, :]
    route_half = route.astype(jnp.bfloat16)
    route_full = route.astype(jnp.float32)
    x_buf = jnp.dot(route_half, tokens, preferred_element_type=jnp.float32).astype(jnp.bfloat16)
    c_buf = jnp.dot(route_half, cotangent, preferred_element_type=jnp.float32).astype(jnp.bfloat16)
    p_buf = jnp.sum(route_full * gate_prob[None, :], axis=1)
    x_buf = x_buf.reshape(experts, capacity, width)
    c_buf = c_buf.reshape(experts, capacity, width)
    p_buf = p_buf.reshape(experts, capacity)
    x_recv, c_recv, p_recv = (
        lax.all_to_all(x_buf, ("wide", "narrow"), split_axis=0, concat_axis=0, tiled=True),
        lax.all_to_all(c_buf, ("wide", "narrow"), split_axis=0, concat_axis=0, tiled=True),
        lax.all_to_all(
            p_buf.astype(jnp.bfloat16), ("wide", "narrow"), split_axis=0, concat_axis=0, tiled=True
        ).astype(p_buf.dtype),
    )
    rows_in = x_recv.reshape(sources * capacity, width)
    rows_cot = c_recv.reshape(sources * capacity, width)
    rows_prob = p_recv.reshape(sources * capacity)
    dx_rows, prob_rows, ggate, gup, gdown = expert_grad(
        rows_in, rows_cot, rows_prob, w_gate[0], w_up[0], w_down[0]
    )
    dx_back, prob_back = (
        lax.all_to_all(
            dx_rows.reshape(sources, capacity, width),
            ("wide", "narrow"),
            split_axis=0,
            concat_axis=0,
            tiled=True,
        ),
        lax.all_to_all(
            prob_rows.reshape(sources, capacity).astype(jnp.bfloat16),
            ("wide", "narrow"),
            split_axis=0,
            concat_axis=0,
            tiled=True,
        ).astype(jnp.float32),
    )
    dx_back = dx_back.reshape(experts * capacity, width)
    prob_back = prob_back.reshape(experts * capacity)
    grad_tokens = lax.dot_general(
        route_half, dx_back, (((0,), (0,)), ((), ())), preferred_element_type=jnp.float32
    ).astype(jnp.bfloat16)
    grad_prob = jnp.sum(route_full * prob_back[:, None], axis=0)
    return (grad_tokens, grad_prob, ggate[None], gup[None], gdown[None])


def solution(mesh):
    return jax.shard_map(
        on_device,
        mesh=mesh,
        in_specs=(
            P(("wide", "narrow"), None),
            P(("wide", "narrow"), None),
            P(("wide", "narrow")),
            P(("wide", "narrow"), None),
            P(("wide", "narrow")),
            P(("wide", "narrow"), None, None),
            P(("wide", "narrow"), None, None),
            P(("wide", "narrow"), None, None),
        ),
        out_specs=(
            P(("wide", "narrow"), None),
            P(("wide", "narrow")),
            P(("wide", "narrow"), None, None),
            P(("wide", "narrow"), None, None),
            P(("wide", "narrow"), None, None),
        ),
        check_vma=False,
    )
```

profile of v0, /device:TPU:0, one launch (start us, length us, event | category | flops | bytes accessed | tf_op | source)
XLA Modules:
  0.0 142.3 jit_solution(8700904184969975794)
XLA Ops:
  0.7 0.8 broadcast_compare_fusion
  1.5 0.9 convert_reduce_fusion
  2.4 0.7 add_select_fusion
  3.1 2.3 %convolution_convert_fusion.3 = bf16[192,2048]{1,0:T(8,128)(2,1)} fusion(bf16[128,2048]{1,0:T(8,128)(2,1)} %param.8, s32[128]{0:T(128)S(1)} %add_select_fusion), kind=kOutput, calls=%fused_computation.21 | convolution fusion | flops 101081088 | bytes 1311232 | tf_op jit(solution)/shard_map/dot_general | solution.py:57
  5.4 2.2 %reshape.84 = bf16[32,6,2048]{2,1,0:T(8,128)(2,1)} reshape(bf16[192,2048]{1,0:T(8,128)(2,1)} %convolution_convert_fusion.3) | data formatting | bytes 1572864 | tf_op jit(solution)/shard_map/reshape | solution.py:60
  7.6 7.4 %all-to-all-start.2 = ((bf16[32,6,2048]{2,1,0:T(8,128)(2,1)}), bf16[32,6,2048]{2,1,0:T(8,128)(2,1)}, u32[]{:S(2)}, u32[]{:S(2)}) async-start(bf16[32,6,2048]{2,1,0:T(8,128)(2,1)} %reshape.84), calls=%async_computation.2 | async-start | bytes 2097152 | tf_op jit(solution)/shard_map/all_to_all | solution.py:64
  15.0 1.2 convolution_convert_fusion.4
  16.2 2.2 %reshape.83 = bf16[32,6,2048]{2,1,0:T(8,128)(2,1)} reshape(bf16[192,2048]{1,0:T(8,128)(2,1)} %convolution_convert_fusion.4) | data formatting | bytes 1572864 | tf_op jit(solution)/shard_map/reshape | solution.py:61
  18.4 21.6 %all-to-all-done.2 = bf16[32,6,2048]{2,1,0:T(8,128)(2,1)} async-done(((bf16[32,6,2048]{2,1,0:T(8,128)(2,1)}), bf16[32,6,2048]{2,1,0:T(8,128)(2,1)}, u32[]{:S(2)}, u32[]{:S(2)}) %all-to-all-start.2) | async-done | bytes 786464 | tf_op jit(solution)/shard_map/all_to_all | solution.py:64
  40.0 4.6 %all-to-all-start.1 = ((bf16[32,6,2048]{2,1,0:T(8,128)(2,1)}), bf16[32,6,2048]{2,1,0:T(8,128)(2,1)}, u32[]{:S(2)}, u32[]{:S(2)}) async-start(bf16[32,6,2048]{2,1,0:T(8,128)(2,1)} %reshape.83), calls=%async_computation.1 | async-start | bytes 2097152 | tf_op jit(solution)/shard_map/all_to_all | solution.py:65
  44.6 2.1 %reshape.85 = bf16[192,2048]{1,0:T(8,128)(2,1)} reshape(bf16[32,6,2048]{2,1,0:T(8,128)(2,1)} %all-to-all-done.2) | data formatting | bytes 1572864 | tf_op jit(solution)/shard_map/reshape | solution.py:70
  46.8 3.1 %fusion.5 = f32[192,704]{1,0:T(8,128)S(1)} fusion(bf16[192,2048]{1,0:T(8,128)(2,1)} %reshape.85, bf16[1,2048,704]{1,2,0:T(8,128)(2,1)} %param.13), kind=kOutput, calls=%fused_computation.8 | convolution fusion | flops 553648128 | bytes 4210688 | tf_op jit(solution)/shard_map/dot_general | solution.py:8
  49.9 0.8 copy-done.5
  50.7 1.9 %multiply_convert_fusion.3 = (bf16[192,704]{1,0:T(8,128)(2,1)S(1)}, f32[192,704]{1,0:T(8,128)}) fusion(f32[192,704]{1,0:T(8,128)S(1)} %fusion.5, bf16[192,2048]{1,0:T(8,128)(2,1)S(1)} %copy-done.3, bf16[1,2048,704]{1,2,0:T(8,128)(2,1)S(1)} %copy-done), kind=kOutput, calls=%fused_computation.28 | convolution fusion | flops 554459136 | bytes 5021696 | tf_op jit(solution)/shard_map/dot_general | solution.py:9
  52.6 17.0 %all-to-all-done.1 = bf16[32,6,2048]{2,1,0:T(8,128)(2,1)} async-done(((bf16[32,6,2048]{2,1,0:T(8,128)(2,1)}), bf16[32,6,2048]{2,1,0:T(8,128)(2,1)}, u32[]{:S(2)}, u32[]{:S(2)}) %all-to-all-start.1) | async-done | bytes 786464 | tf_op jit(solution)/shard_map/all_to_all | solution.py:65
  69.7 2.4 %reshape.89 = f32[192,2048]{1,0:T(8,128)} reshape(bf16[32,6,2048]{2,1,0:T(8,128)(2,1)} %all-to-all-done.1) | data formatting | bytes 2359296 | tf_op jit(solution)/shard_map/convert_element_type | solution.py:15
  72.0 3.2 %fusion.24 = bf16[192]{0:T(256)(128)(2,1)S(1)} fusion(f32[192,2048]{1,0:T(8,128)} %reshape.89, bf16[192,704]{1,0:T(8,128)(2,1)S(1)} %get-tuple-element.9, bf16[1,704,2048]{2,1,0:T(8,128)(2,1)} %param.15), kind=kOutput, calls=%fused_computation.26 | convolution fusion | flops 554434368 | bytes 4727168 | tf_op jit(solution)/shard_map/dot_general | solution.py:13
  75.3 11.4 %all_to_all.27 = bf16[32,1,6]{2,1,0:T(2,128)(2,1)S(1)} all-to-all(bf16[32,1,6]{2,1,0:T(2,128)(2,1)S(1)} %convert_element_type.137), channel_id=1, replica_groups=mesh['wide'=8,'narrow'=4] {'wide','narrow'}, dimensions={0} | all-to-all | bytes 768 | tf_op jit(solution)/shard_map/all_to_all | solution.py:84
  87.6 8.9 %all_to_all.28 = bf16[32,1,6]{2,1,0:T(2,128)(2,1)S(1)} all-to-all(bf16[32,1,6]{2,1,0:T(2,128)(2,1)S(1)} %convert_element_type.136), channel_id=1, replica_groups=mesh['wide'=8,'narrow'=4] {'wide','narrow'}, dimensions={0} | all-to-all | bytes 768 | tf_op jit(solution)/shard_map/all_to_all | solution.py:66
  96.5 2.4 %multiply_convert_fusion = bf16[32,6,2048]{2,1,0:T(8,128)(2,1)} fusion(f32[32,6]{1,0:T(8,128)S(1)} %bitcast.50, bf16[32,6,2048]{2,1,0:T(8,128)(2,1)} %all-to-all-done.1), kind=kLoop, calls=%fused_computation.24 | loop fusion | flops 1179648 | bytes 1573632 | tf_op jit(solution)/shard_map/convert_element_type | solution.py:15
  99.0 2.1 %convert_element_type.113 = bf16[192,2048]{1,0:T(8,128)(2,1)} reshape(bf16[32,6,2048]{2,1,0:T(8,128)(2,1)} %multiply_convert_fusion) | data formatting | bytes 1572864 | tf_op jit(solution)/shard_map/convert_element_type | solution.py:15
  101.1 3.6 %multiply_convert_fusion.4 = (bf16[192,704]{1,0:T(8,128)(2,1)S(1)}, bf16[192,704]{1,0:T(8,128)(2,1)S(1)}) fusion(f32[192,704]{1,0:T(8,128)} %copy-done.5, f32[192,704]{1,0:T(8,128)} %get-tuple-element.10, bf16[192,2048]{1,0:T(8,128)(2,1)} %convert_element_type.113, bf16[1,704,2048]{2,1,0:T(8,128)(2,1)} %param.15), kind=kOutput, calls=%fused_computation.29 | convolution fusion | flops 555405312 | bytes 5292032 | tf_op jit(solution)/shard_map/dot_general | solution.py:19
  104.8 0.8 fusion.3
  105.6 1.7 %fusion.21 = bf16[192,2048]{1,0:T(8,128)(2,1)} fusion(f32[192,2048]{1,0:T(8,128)S(1)} %fusion.3, bf16[192,704]{1,0:T(8,128)(2,1)S(1)} %get-tuple-element.7, bf16[1,2048,704]{1,2,0:T(8,128)(2,1)S(1)} %copy-done), kind=kOutput, calls=%fused_computation.20 | convolution fusion | flops 554434560 | bytes 5513216 | tf_op jit(solution)/shard_map/dot_general | solution.py:33
  107.2 2.2 %reshape.86 = bf16[32,6,2048]{2,1,0:T(8,128)(2,1)} reshape(bf16[192,2048]{1,0:T(8,128)(2,1)} %fusion.21) | data formatting | bytes 1572864 | tf_op jit(solution)/shard_map/reshape | solution.py:78
  109.5 3.6 %all-to-all-start.3 = ((bf16[32,6,2048]{2,1,0:T(8,128)(2,1)}), bf16[32,6,2048]{2,1,0:T(8,128)(2,1)}, u32[]{:S(2)}, u32[]{:S(2)}) async-start(bf16[32,6,2048]{2,1,0:T(8,128)(2,1)} %reshape.86), calls=%async_computation.3 | async-start | bytes 2097152 | tf_op jit(solution)/shard_map/all_to_all | solution.py:77
  113.2 3.8 %fusion.1 = bf16[1,2048,704]{1,2,0:T(8,128)(2,1)} fusion(bf16[192,2048]{1,0:T(8,128)(2,1)} %reshape.85, bf16[192,704]{1,0:T(8,128)(2,1)S(1)} %get-tuple-element.7), kind=kOutput, calls=%fused_computation.4 | convolution fusion | flops 555089920 | bytes 3940352 | tf_op jit(solution)/shard_map/dot_general | solution.py:27
  117.0 2.5 %fusion = bf16[1,2048,704]{1,2,0:T(8,128)(2,1)} fusion(bf16[192,2048]{1,0:T(8,128)(2,1)S(1)} %copy-done.4, bf16[192,704]{1,0:T(8,128)(2,1)S(1)} %copy-done.8), kind=kOutput, calls=%fused_computation.3 | convolution fusion | flops 555089920 | bytes 3940352 | tf_op jit(solution)/shard_map/dot_general | solution.py:24
  119.5 2.6 %fusion.2 = bf16[1,704,2048]{2,1,0:T(8,128)(2,1)} fusion(bf16[192,704]{1,0:T(8,128)(2,1)S(1)} %get-tuple-element.9, f32[192,2048]{1,0:T(8,128)S(1)} %copy-done.1, f32[192]{0:T(256)S(1)} %reshape.91), kind=kOutput, calls=%fused_computation.5 | convolution fusion | flops 555876352 | bytes 4727552 | tf_op jit(solution)/shard_map/dot_general | solution.py:16
  122.1 15.8 %all-to-all-done.3 = bf16[32,6,2048]{2,1,0:T(8,128)(2,1)} async-done(((bf16[32,6,2048]{2,1,0:T(8,128)(2,1)}), bf16[32,6,2048]{2,1,0:T(8,128)(2,1)}, u32[]{:S(2)}, u32[]{:S(2)}) %all-to-all-start.3) | async-done | bytes 786464 | tf_op jit(solution)/shard_map/all_to_all | solution.py:77
  137.9 2.2 %reshape.87 = bf16[192,2048]{1,0:T(8,128)(2,1)} reshape(bf16[32,6,2048]{2,1,0:T(8,128)(2,1)} %all-to-all-done.3) | data formatting | bytes 1572864 | tf_op jit(solution)/shard_map/reshape | solution.py:92
  140.0 2.3 %convolution_convert_fusion.5 = bf16[128,2048]{1,0:T(8,128)(2,1)} fusion(bf16[192,2048]{1,0:T(8,128)(2,1)} %reshape.87, s32[128]{0:T(128)S(1)} %add_select_fusion), kind=kOutput, calls=%fused_computation.23 | convolution fusion | flops 100950016 | bytes 1311232 | tf_op jit(solution)/shard_map/dot_general | solution.py:94
  (27 shorter events, 1.2 us)
Async XLA Ops:
  0.6 50.1 %copy-start = (bf16[1,2048,704]{1,2,0:T(8,128)(2,1)S(1)}, bf16[1,2048,704]{1,2,0:T(8,128)(2,1)}, u32[]{:S(2)}) copy-start(bf16[1,2048,704]{1,2,0:T(8,128)(2,1)} %param.14) | copy-start | bytes 8650756
  0.6 14.3 %copy-start.6 = (bf16[128,2048]{1,0:T(8,128)(2,1)S(1)}, bf16[128,2048]{1,0:T(8,128)(2,1)}, u32[]{:S(2)}) copy-start(bf16[128,2048]{1,0:T(8,128)(2,1)} %param.9) | copy-start | bytes 1572868
  7.6 32.5 %all-to-all-start.2 = ((bf16[32,6,2048]{2,1,0:T(8,128)(2,1)}), bf16[32,6,2048]{2,1,0:T(8,128)(2,1)}, u32[]{:S(2)}, u32[]{:S(2)}) async-start(bf16[32,6,2048]{2,1,0:T(8,128)(2,1)} %reshape.84), calls=%async_computation.2 | async-start | bytes 2097152 | tf_op jit(solution)/shard_map/all_to_all | solution.py:64
  40.0 29.6 %all-to-all-start.1 = ((bf16[32,6,2048]{2,1,0:T(8,128)(2,1)}), bf16[32,6,2048]{2,1,0:T(8,128)(2,1)}, u32[]{:S(2)}, u32[]{:S(2)}) async-start(bf16[32,6,2048]{2,1,0:T(8,128)(2,1)} %reshape.83), calls=%async_computation.1 | async-start | bytes 2097152 | tf_op jit(solution)/shard_map/all_to_all | solution.py:65
  46.8 4.0 %copy-start.3 = (bf16[192,2048]{1,0:T(8,128)(2,1)S(1)}, bf16[192,2048]{1,0:T(8,128)(2,1)}, u32[]{:S(2)}) copy-start(bf16[192,2048]{1,0:T(8,128)(2,1)} %reshape.85) | copy-start | bytes 2359300
  49.9 0.8 copy-start.5
  72.0 14.9 %copy-start.9 = (f32[128]{0:T(128)S(1)}, f32[128]{0:T(128)}, u32[]{:S(2)}) copy-start(f32[128]{0:T(128)} %param.10) | copy-start | bytes 1540
  101.1 3.6 %copy-start.2 = (bf16[1,2048,704]{1,2,0:T(8,128)(2,1)S(1)}, bf16[1,2048,704]{1,2,0:T(8,128)(2,1)}, u32[]{:S(2)}) copy-start(bf16[1,2048,704]{1,2,0:T(8,128)(2,1)} %param.13) | copy-start | bytes 8650756
  104.7 0.8 copy-start.7
  109.5 28.4 %all-to-all-start.3 = ((bf16[32,6,2048]{2,1,0:T(8,128)(2,1)}), bf16[32,6,2048]{2,1,0:T(8,128)(2,1)}, u32[]{:S(2)}, u32[]{:S(2)}) async-start(bf16[32,6,2048]{2,1,0:T(8,128)(2,1)} %reshape.86), calls=%async_computation.3 | async-start | bytes 2097152 | tf_op jit(solution)/shard_map/all_to_all | solution.py:77
  113.2 3.8 %copy-start.4 = (bf16[192,2048]{1,0:T(8,128)(2,1)S(1)}, bf16[192,2048]{1,0:T(8,128)(2,1)}, u32[]{:S(2)}) copy-start(bf16[192,2048]{1,0:T(8,128)(2,1)} %reshape.85) | copy-start | bytes 2359300
  113.2 3.8 %copy-start.8 = (bf16[192,704]{1,0:T(8,128)(2,1)S(1)}, bf16[192,704]{1,0:T(8,128)(2,1)}, u32[]{:S(2)}) copy-start(bf16[192,704]{1,0:T(8,128)(2,1)} %copy-done.7) | copy-start | bytes 811012
  117.0 2.5 %copy-start.1 = (f32[192,2048]{1,0:T(8,128)S(1)}, f32[192,2048]{1,0:T(8,128)}, u32[]{:S(2)}) copy-start(f32[192,2048]{1,0:T(8,128)} %reshape.89) | copy-start | bytes 4718596
where the time goes:
time: 144 us; the launch traced here: 142 us
  waiting for transfers between devices  54.4 us (38%)
  matrix products  28.9 us (20%)
  blocking collectives  20.3 us (14%)
  local copies, waits for them, and re-layouts  16.7 us (12%)
  starting transfers between devices  15.6 us (11%)
  other arithmetic  5.64 us (4%)
    all_to_all x1, waiting for transfers between devices, on_device(): lax.all_to_all(x_buf, ('wide', 'narrow'), split_axis=0, concat_axis=0, ti...  21.6 us
    all_to_all x1, waiting for transfers between devices, on_device(): lax.all_to_all(c_buf, ('wide', 'narrow'), split_axis=0, concat_axis=0, ti...  17 us
    all_to_all x1, waiting for transfers between devices, on_device(): lax.all_to_all(dx_rows.reshape(sources, capacity, width), ('wide', 'narro...  15.8 us
    all_to_all x1, blocking collectives, on_device(): lax.all_to_all(prob_rows.reshape(sources, capacity).astype(jnp.bfloat16),...  11.4 us
    all_to_all x1, blocking collectives, on_device(): lax.all_to_all(p_buf.astype(jnp.bfloat16), ('wide', 'narrow'), split_axis...  8.87 us
    all_to_all x1, starting transfers between devices, on_device(): lax.all_to_all(x_buf, ('wide', 'narrow'), split_axis=0, concat_axis=0, ti...  7.43 us
    all_to_all x1, starting transfers between devices, on_device(): lax.all_to_all(c_buf, ('wide', 'narrow'), split_axis=0, concat_axis=0, ti...  4.58 us
    dot_general x1, matrix products, expert_grad(): lax.dot_general(rows_in, dup, (((0,), (0,)), ((), ())), preferred_element...  3.76 us
  transfers between devices with their start and end apart: 3, of which 3 were waited for; matrix products, arithmetic and copies ran while one was open for 14% of the time, Pallas kernels for 0%

commit v1 on v0

v1 whole, which is shorter than its diff:
```python
import functools

import jax
import jax.numpy as jnp
import numpy as np
from jax import lax
from jax.experimental import pallas as pl
from jax.experimental.pallas import tpu as pltpu
from jax.sharding import PartitionSpec as P

GROUP = 8
PIECES = 8
MESH = pl.DeviceIdType.MESH
NT = (((1,), (1,)), ((), ()))
TN = (((0,), (0,)), ((), ()))


def f32dot(a, b, dims=(((1,), (0,)), ((), ()))):
    return lax.dot_general(a, b, dims, preferred_element_type=jnp.float32)


def exchange_kernel(
    n, n_narrow, cap,
    tok_ref, cot_ref, prob_ref, tgt_row_ref, tgt_ref, eid_ref, slot_ref, perm_ref,
    wg_hbm, wu_hbm, wd_hbm,
    gtok_ref, gprob_ref, x_ref, d_ref, h_ref, dg_ref, du_ref,
    wg, wu, wd, xstack, dstack, cstack,
    xsend, dsend, bsend, xrecv, drecv, brecv, psend, precv, pmat,
    wsem, xs, xr, ds, dr, bs, br, ps, pr,
):
    wide, narrow = lax.axis_index("wide"), lax.axis_index("narrow")
    me = wide * n_narrow + narrow
    groups = n // GROUP
    mine = me // GROUP
    lane = me % GROUP
    tok = tok_ref.shape[0]
    piece = tok_ref.shape[1] // PIECES
    rows = GROUP * cap
    block = cap * PIECES

    loads = [
        pltpu.make_async_copy(src, dst, wsem.at[i])
        for i, (src, dst) in enumerate(((wg_hbm, wg), (wu_hbm, wu), (wd_hbm, wd)))
    ]
    for load in loads:
        load.start()

    def where(d):
        return (d // n_narrow, d % n_narrow)

    barrier = pltpu.get_barrier_semaphore()

    @pl.loop(1, n)
    def _(i):
        pl.semaphore_signal(
            barrier, inc=1, device_id=where((me + i) % n), device_id_type=MESH
        )

    for k in range(PIECES):
        cols = slice(k * piece, (k + 1) * piece)
        at = slice(k * tok, (k + 1) * tok)
        xstack[at, :] = tok_ref[:, cols]
        dstack[at, :] = (prob_ref[...] * cot_ref[:, cols].astype(jnp.float32)).astype(
            jnp.bfloat16
        )

    def copy(send, recv, ss, rs, d):
        return pltpu.make_async_remote_copy(
            src_ref=send.at[d], dst_ref=recv.at[me], send_sem=ss.at[d],
            recv_sem=rs.at[me], device_id=where(d), device_id_type=MESH,
        )

    def arrival(send, recv, ss, rs, s):
        return pltpu.make_async_remote_copy(
            src_ref=send.at[s], dst_ref=recv.at[s], send_sem=ss.at[s],
            recv_sem=rs.at[s], device_id=where(s), device_id_type=MESH,
        )

    def fill(i, first):
        g = (mine - i + groups) % groups
        base = g * GROUP
        at = lax.broadcasted_iota(jnp.int32, (GROUP * block, tok), 0) + base * block
        route = jnp.concatenate(
            [
                (at == tgt_row_ref[...] + k).astype(jnp.float32).astype(jnp.bfloat16)
                for k in range(PIECES)
            ],
            axis=1,
        )
        xsend[pl.ds(base, GROUP)] = (
            f32dot(route, xstack[...]).astype(jnp.bfloat16).reshape(GROUP, block, piece)
        )
        dsend[pl.ds(base, GROUP)] = (
            f32dot(route, dstack[...]).astype(jnp.bfloat16).reshape(GROUP, block, piece)
        )
        if first:
            pl.semaphore_wait(barrier, n - 1)

        for send, recv, ss, rs in ((xsend, xrecv, xs, xr), (dsend, drecv, ds, dr)):

            @pl.loop(0, GROUP)
            def _(q):
                d = base + (lane + q) % GROUP

                @pl.when(d != me)
                def _():
                    copy(send, recv, ss, rs, d).start()

    fill(0, True)
    xrecv[me] = xsend[me]
    drecv[me] = dsend[me]

    @pl.loop(1, groups)
    def _(i):
        fill(i, False)

    for load in loads:
        load.wait()

    spread = lax.broadcasted_iota(jnp.int32, (rows, 128), 0) % cap
    keep = spread == lax.broadcasted_iota(jnp.int32, (rows, 128), 1)
    owner = lax.broadcasted_iota(jnp.int32, (GROUP, rows), 1) // cap
    gather = (owner == lax.broadcasted_iota(jnp.int32, (GROUP, rows), 0)).astype(jnp.float32)

    def take(send, recv, ss, rs, base, out_ref, at):
        @pl.loop(0, GROUP)
        def _(q):
            s = base + q

            @pl.when(s != me)
            def _():
                arrival(send, recv, ss, rs, s).wait_recv()

        got = recv[pl.ds(base, GROUP)].reshape(GROUP * block, piece)
        got = f32dot(perm_ref[...], got).astype(jnp.bfloat16)
        for k in range(PIECES):
            out_ref[at, k * piece:(k + 1) * piece] = got[k * rows:(k + 1) * rows]

    @pl.loop(0, groups)
    def _(i):
        base = ((mine + i) % groups) * GROUP
        at = pl.ds(pl.multiple_of(i * rows, rows), rows)
        take(xsend, xrecv, xs, xr, base, x_ref, at)
        x = x_ref[at, :]
        g = f32dot(x, wg[...])
        u = f32dot(x, wu[...])
        sig = 1.0 / (1.0 + jnp.exp(-g))
        silu = g * sig
        h = (silu * u).astype(jnp.bfloat16)
        h_ref[at, :] = h
        take(dsend, drecv, ds, dr, base, d_ref, at)
        dh = f32dot(d_ref[at, :], wd[...], NT)
        total = jnp.sum(h.astype(jnp.float32) * dh, axis=1, keepdims=True)
        dg = (dh * u * sig * (1.0 + g * (1.0 - sig))).astype(jnp.bfloat16)
        du = (dh * silu).astype(jnp.bfloat16)
        dg_ref[at, :] = dg
        du_ref[at, :] = du
        dx = (f32dot(dg, wg[...], NT) + f32dot(du, wu[...], NT)).astype(jnp.bfloat16)
        for k in range(PIECES):
            cstack[k * rows:(k + 1) * rows, :] = dx[:, k * piece:(k + 1) * piece]
        bsend[pl.ds(base, GROUP)] = (
            f32dot(perm_ref[...], cstack[...], TN)
            .astype(jnp.bfloat16)
            .reshape(GROUP, block, piece)
        )
        probs = lax.dot_general(
            gather, jnp.where(keep, total, 0.0), (((1,), (0,)), ((), ())),
            precision=lax.Precision.HIGHEST, preferred_element_type=jnp.float32,
        )
        for q in range(GROUP):
            psend[base + q] = probs[q:q + 1]

        @pl.loop(0, GROUP)
        def _(q):
            d = base + (lane + q) % GROUP

            @pl.when(d != me)
            def _():
                copy(bsend, brecv, bs, br, d).start()
                copy(psend, precv, ps, pr, d).start()

        @pl.when(i == 0)
        def _():
            brecv[me] = bsend[me]
            precv[me] = psend[me]

    @pl.loop(0, n)
    def _(s):
        @pl.when(s != me)
        def _():
            arrival(bsend, brecv, bs, br, s).wait_recv()
            arrival(psend, precv, ps, pr, s).wait_recv()

        pmat[pl.ds(s, 1), :] = precv[s]

    back = brecv[...].reshape(n * block, piece)
    at = lax.broadcasted_iota(jnp.int32, (tok, n * block), 1)
    for k in range(PIECES):
        route = (at == tgt_ref[...] + k).astype(jnp.float32).astype(jnp.bfloat16)
        gtok_ref[:, k * piece:(k + 1) * piece] = f32dot(route, back).astype(jnp.bfloat16)
    pick = (lax.broadcasted_iota(jnp.int32, (tok, n), 1) == eid_ref[...]).astype(jnp.float32)
    found = lax.dot_general(
        pick, pmat[...], (((1,), (0,)), ((), ())),
        precision=lax.Precision.HIGHEST, preferred_element_type=jnp.float32,
    )
    found = jnp.where(
        lax.broadcasted_iota(jnp.int32, (tok, 128), 1) == slot_ref[...], found, 0.0
    )
    gprob_ref[...] = jnp.sum(found, axis=1, keepdims=True) / prob_ref[...]

    @pl.loop(0, n)
    def _(d):
        @pl.when(d != me)
        def _():
            copy(xsend, xrecv, xs, xr, d).wait_send()
            copy(dsend, drecv, ds, dr, d).wait_send()
            copy(bsend, brecv, bs, br, d).wait_send()
            copy(psend, precv, ps, pr, d).wait_send()


def weight_kernel(x_ref, d_ref, h_ref, dg_ref, du_ref, gg_ref, gu_ref, gd_ref):
    x = x_ref[...]
    gg_ref[0] = f32dot(x, dg_ref[...], TN).astype(jnp.bfloat16)
    gu_ref[0] = f32dot(x, du_ref[...], TN).astype(jnp.bfloat16)
    gd_ref[0] = f32dot(h_ref[...], d_ref[...], TN).astype(jnp.bfloat16)


def on_device(tokens, cotangent, gate_prob, expert_ids, keep_mask, w_gate, w_up, w_down):
    tok, width = tokens.shape
    hidden = w_gate.shape[2]
    n_wide, n_narrow = lax.axis_size("wide"), lax.axis_size("narrow")
    n = n_wide * n_narrow
    cap = max(2, 5 * tok // (4 * n) + 1)
    piece = width // PIECES
    block = cap * PIECES
    rows = GROUP * cap

    ids = expert_ids[:, 0]
    kept = keep_mask == 1
    order = jnp.arange(tok, dtype=jnp.int32)
    earlier = (ids[:, None] == ids[None, :]) & kept[None, :] & (order[None, :] < order[:, None])
    slot = jnp.sum(earlier.astype(jnp.int32), axis=1)
    target = jnp.where(kept, ids * block + slot * PIECES, -block)
    owner = jnp.where(kept, ids, -1)

    r = np.arange(GROUP * block)
    source, rest = r // block, r % block
    perm = np.zeros((GROUP * block, GROUP * block), np.float32)
    perm[(rest % PIECES) * rows + source * cap + rest // PIECES, r] = 1.0

    vmem = pl.BlockSpec(memory_space=pltpu.VMEM)
    hbm = pl.BlockSpec(memory_space=pl.ANY)
    bf16, f32 = jnp.bfloat16, jnp.float32
    buf = pltpu.VMEM((n, block, piece), bf16)
    small = pltpu.VMEM((n, 1, 128), f32)
    gtok, gprob, x, d, h, dg, du = pl.pallas_call(
        functools.partial(exchange_kernel, n, n_narrow, cap),
        out_shape=(
            jax.ShapeDtypeStruct((tok, width), bf16),
            jax.ShapeDtypeStruct((tok, 1), f32),
            jax.ShapeDtypeStruct((n * cap, width), bf16),
            jax.ShapeDtypeStruct((n * cap, width), bf16),
            jax.ShapeDtypeStruct((n * cap, hidden), bf16),
            jax.ShapeDtypeStruct((n * cap, hidden), bf16),
            jax.ShapeDtypeStruct((n * cap, hidden), bf16),
        ),
        in_specs=[vmem] * 8 + [hbm] * 3,
        out_specs=(vmem,) * 7,
        scratch_shapes=[
            pltpu.VMEM((width, hidden), bf16),
            pltpu.VMEM((width, hidden), bf16),
            pltpu.VMEM((hidden, width), bf16),
            pltpu.VMEM((PIECES * tok, piece), bf16),
            pltpu.VMEM((PIECES * tok, piece), bf16),
            pltpu.VMEM((GROUP * block, piece), bf16),
            buf, buf, buf, buf, buf, buf, small, small,
            pltpu.VMEM((n, 128), f32),
            pltpu.SemaphoreType.DMA((3,)),
        ] + [pltpu.SemaphoreType.DMA((n,))] * 8,
        compiler_params=pltpu.CompilerParams(
            collective_id=0, has_side_effects=True, vmem_limit_bytes=48 * 1024 * 1024
        ),
        name="exchange",
    )(
        tokens, cotangent, gate_prob[:, None], target[None, :], target[:, None],
        owner[:, None], slot[:, None], jnp.asarray(perm, bf16),
        w_gate[0], w_up[0], w_down[0],
    )

    tile = 256
    full = pl.BlockSpec((n * cap, hidden), lambda i: (0, 0))
    part = pl.BlockSpec((n * cap, tile), lambda i: (0, i))
    ggate, gup, gdown = pl.pallas_call(
        weight_kernel,
        grid=(width // tile,),
        out_shape=(
            jax.ShapeDtypeStruct((1, width, hidden), bf16),
            jax.ShapeDtypeStruct((1, width, hidden), bf16),
            jax.ShapeDtypeStruct((1, hidden, width), bf16),
        ),
        in_specs=[part, part, full, full, full],
        out_specs=(
            pl.BlockSpec((1, tile, hidden), lambda i: (0, i, 0)),
            pl.BlockSpec((1, tile, hidden), lambda i: (0, i, 0)),
            pl.BlockSpec((1, hidden, tile), lambda i: (0, 0, i)),
        ),
        compiler_params=pltpu.CompilerParams(vmem_limit_bytes=32 * 1024 * 1024),
        name="weights",
    )(x, d, h, dg, du)
    return gtok, gprob[:, 0], ggate, gup, gdown


def solution(mesh):
    both = ("wide", "narrow")
    return jax.shard_map(
        on_device,
        mesh=mesh,
        in_specs=(
            P(both, None), P(both, None), P(both), P(both, None), P(both),
            P(both, None, None), P(both, None, None), P(both, None, None),
        ),
        out_specs=(
            P(both, None), P(both),
            P(both, None, None), P(both, None, None), P(both, None, None),
        ),
        check_vma=False,
    )
```

time: 144 us -> 103 us (0.72)
  Pallas kernels: 0 us -> 69.1 us
  waiting for transfers between devices: 54.4 us -> 0 us
  matrix products: 28.9 us -> 0 us
  blocking collectives: 20.3 us -> 0 us
  starting transfers between devices: 15.6 us -> 0 us
  local copies, waits for them, and re-layouts: 16.7 us -> 29.3 us
  other arithmetic: 5.64 us -> 2.87 us
    pallas_call x0 -> x2, Pallas kernels: none -> 69.1 us  [the longest x1 63.6 us: on_device(): pl.pallas_call(functools.partial(exchange_kernel, n, n_narrow, cap), out_...]
    all_to_all x3 -> x0, waiting for transfers between devices: 54.4 us -> none  [the longest x1 21.6 us: on_device(): lax.all_to_all(x_buf, ('wide', 'narrow'), split_axis=0, concat_axis=0, ti...]
    dot_general x12 -> x0, matrix products: 28.9 us -> none  [the longest x1 3.76 us: expert_grad(): lax.dot_general(rows_in, dup, (((0,), (0,)), ((), ())), preferred_element...]
    unnamed x20 -> x31, local copies, waits for them, and re-layouts: 0.87 us -> 28.2 us
    all_to_all x2 -> x0, blocking collectives: 20.3 us -> none  [the longest x1 11.4 us: on_device(): lax.all_to_all(prob_rows.reshape(sources, capacity).astype(jnp.bfloat16),...]
    all_to_all x3 -> x0, starting transfers between devices: 15.6 us -> none  [the longest x1 7.43 us: on_device(): lax.all_to_all(x_buf, ('wide', 'narrow'), split_axis=0, concat_axis=0, ti...]
    reshape x5 -> x0, local copies, waits for them, and re-layouts: 10.9 us -> none  [the longest x1 2.23 us: on_device(): dx_rows.reshape(sources, capacity, width)]
    convert_element_type x6 -> x0, local copies, waits for them, and re-layouts: 4.93 us -> none  [the longest x1 2.37 us: expert_grad(): rows_cot.astype(jnp.float32)]
  transfers between devices with their start and end apart: 3 -> 0, of which waited for: 3 -> 0; matrix products, arithmetic and copies ran while one was open for 14% -> 0% of each run, Pallas kernels for 0% -> 0%
where the time goes in v1:
time: 103 us; the launch traced here: 102 us
  Pallas kernels  69.1 us (67%)
  local copies, waits for them, and re-layouts  29.3 us (28%)
  other arithmetic  2.87 us (3%)
    pallas_call x1, Pallas kernels, on_device(): pl.pallas_call(functools.partial(exchange_kernel, n, n_narrow, cap), out_...  63.6 us
    unnamed x31, local copies, waits for them, and re-layouts  28.2 us
    pallas_call x1, Pallas kernels, on_device(): pl.pallas_call(weight_kernel, grid=(width // tile,), out_shape=(jax.Shape...  5.53 us

profile of v1, /device:TPU:0, one launch (start us, length us, event | category | flops | bytes accessed | tf_op | source)
XLA Modules:
  0.0 102.0 jit_solution(1355370583082531338)
XLA Ops:
  0.6 0.7 broadcast_compare_fusion
  1.3 0.9 convert_reduce_fusion
  2.2 0.7 select_bitcast_fusion
  2.9 0.1 copy.34.eid_ref
  3.0 0.1 copy.33.tgt_ref
  3.1 0.1 copy.35.slot_ref
  3.2 0.8 copy.32.prob_ref
  4.0 4.6 %copy.30 = bf16[1,2048,704]{2,1,0:T(8,128)(2,1)} copy(bf16[1,2048,704]{1,2,0:T(8,128)(2,1)} %param.14) | data formatting | bytes 5767168 | tf_op args[5]
  8.6 0.0 copy-start.6
  8.6 0.0 copy-start.7
  8.6 0.0 copy-start.8
  8.6 4.7 %copy.31 = bf16[1,2048,704]{2,1,0:T(8,128)(2,1)} copy(bf16[1,2048,704]{1,2,0:T(8,128)(2,1)} %param.15) | data formatting | bytes 5767168 | tf_op args[6]
  13.3 0.0 copy-done.6
  13.3 0.0 copy-done.7
  13.3 0.0 copy-done.8
  13.3 63.6 %exchange.1 = (bf16[128,2048]{1,0:T(8,128)(2,1)S(1)}, f32[128,1]{1,0:T(8,128)S(1)}, bf16[192,2048]{1,0:T(8,128)(2,1)S(1)}, bf16[192,2048]{1,0:T(8,128)(2,1)S(1)}...) custom-call(bf16[128,2048]{1,0:T(8,128)(2,1)S(1)} %copy-done.6, ...), custom_call_target="tpu_custom_call" | custom-call | tf_op jit(solution)/shard_map/exchange/pallas_call | solution.py:256
  76.9 0.0 copy-start.1
  76.9 0.9 copy-done.1
  77.8 0.9 copy-done.3
  78.7 0.8 copy-done.5
  79.5 0.7 copy-done.9
  80.2 0.7 copy-done.11
  80.9 0.6 reduce
  81.5 1.1 %copy-done.2 = bf16[192,2048]{1,0:T(8,128)(2,1)S(1)} copy-done((bf16[192,2048]{1,0:T(8,128)(2,1)S(1)}, bf16[192,2048]{1,0:T(8,128)(2,1)}, u32[]{:S(2)}) %copy-start.2) | copy-done | bytes 786456
  82.7 1.1 %copy-done.4 = bf16[192,2048]{1,0:T(8,128)(2,1)S(1)} copy-done((bf16[192,2048]{1,0:T(8,128)(2,1)S(1)}, bf16[192,2048]{1,0:T(8,128)(2,1)}, u32[]{:S(2)}) %copy-start.4) | copy-done | bytes 786456
  83.8 1.0 copy-done.10
  84.8 1.0 copy-done.12
  85.7 5.5 %weights.1 = (bf16[1,2048,704]{2,1,0:T(8,128)(2,1)S(1)}, bf16[1,2048,704]{2,1,0:T(8,128)(2,1)S(1)}, bf16[1,704,2048]{2,1,0:T(8,128)(2,1)}) custom-call(bf16[192,2048]{1,0:T(8,128)(2,1)S(1)} %copy-done.2, bf16[192,2048]{1,0:T(8,128)(2,1)S(1)} %copy-done.4, bf16[192,704]{1,0:T(8,128)(2,1)S(1)} %get-tuple-element.19.h_ref, bf16[192,704]{1,0:T(8,128)(2,1)S(1)} %copy-done.10, ...), custom_call_target="tpu_custom_call" | custom-call | tf_op jit(solution)/shard_map/weights/pallas_call | solution.py:293
  91.3 1.6 %copy-done = bf16[1,2048,704]{2,1,0:T(8,128)(2,1)} copy-done((bf16[1,2048,704]{2,1,0:T(8,128)(2,1)}, bf16[1,2048,704]{2,1,0:T(8,128)(2,1)S(1)}, u32[]{:S(2)}) %copy-start) | copy-done | bytes 2883608
  92.9 4.6 %copy.36 = bf16[1,2048,704]{1,2,0:T(8,128)(2,1)} copy(bf16[1,2048,704]{2,1,0:T(8,128)(2,1)} %copy-done) | data formatting | bytes 5767168
  97.5 2.7 %copy.37 = bf16[1,2048,704]{1,2,0:T(8,128)(2,1)} copy(bf16[1,2048,704]{2,1,0:T(8,128)(2,1)S(1)} %get-tuple-element.38) | data formatting | bytes 5767168
  100.1 1.9 %copy.39 = bf16[128,2048]{1,0:T(8,128)(2,1)} copy(bf16[128,2048]{1,0:T(8,128)(2,1)} %copy-done.5) | data formatting | bytes 1048576
  (9 shorter events, 0.0 us)
Async XLA Ops:
  8.6 4.7 %copy-start.6 = (bf16[128,2048]{1,0:T(8,128)(2,1)S(1)}, bf16[128,2048]{1,0:T(8,128)(2,1)}, u32[]{:S(2)}) copy-start(bf16[128,2048]{1,0:T(8,128)(2,1)} %tok_ref.1) | copy-start | bytes 1572868
  8.6 4.7 %copy-start.7 = (bf16[128,2048]{1,0:T(8,128)(2,1)S(1)}, bf16[128,2048]{1,0:T(8,128)(2,1)}, u32[]{:S(2)}) copy-start(bf16[128,2048]{1,0:T(8,128)(2,1)} %cot_ref.1) | copy-start | bytes 1572868
  8.6 4.7 %copy-start.8 = (bf16[384,384]{1,0:T(8,128)(2,1)S(1)}, bf16[384,384]{1,0:T(8,128)(2,1)}, u32[]{:S(2)}) copy-start(bf16[384,384]{1,0:T(8,128)(2,1)} %constant.14.clone.perm_ref) | copy-start | bytes 884740
  76.9 0.9 copy-start.1
  77.8 0.9 copy-start.3
  78.7 0.8 copy-start.5
  79.5 0.7 copy-start.9
  80.2 0.7 copy-start.11
  81.5 1.1 %copy-start.2 = (bf16[192,2048]{1,0:T(8,128)(2,1)S(1)}, bf16[192,2048]{1,0:T(8,128)(2,1)}, u32[]{:S(2)}) copy-start(bf16[192,2048]{1,0:T(8,128)(2,1)} %copy-done.1) | copy-start | bytes 2359300
  82.7 1.1 %copy-start.4 = (bf16[192,2048]{1,0:T(8,128)(2,1)S(1)}, bf16[192,2048]{1,0:T(8,128)(2,1)}, u32[]{:S(2)}) copy-start(bf16[192,2048]{1,0:T(8,128)(2,1)} %copy-done.3) | copy-start | bytes 2359300
  83.8 1.0 copy-start.10
  84.8 1.0 copy-start.12
  91.3 1.6 %copy-start = (bf16[1,2048,704]{2,1,0:T(8,128)(2,1)}, bf16[1,2048,704]{2,1,0:T(8,128)(2,1)S(1)}, u32[]{:S(2)}) copy-start(bf16[1,2048,704]{2,1,0:T(8,128)(2,1)S(1)} %get-tuple-element.37) | copy-start | bytes 8650756

commit v2 on v1

--- a/solution.py
+++ b/solution.py
@@ -21,10 +21,10 @@
 
 def exchange_kernel(
     n, n_narrow, cap,
-    tok_ref, cot_ref, prob_ref, tgt_row_ref, tgt_ref, eid_ref, slot_ref, perm_ref,
+    tok_ref, cot_ref, prob_ref, ids_ref, keep_ref, perm_ref, unperm_ref,
     wg_hbm, wu_hbm, wd_hbm,
-    gtok_ref, gprob_ref, x_ref, d_ref, h_ref, dg_ref, du_ref,
-    wg, wu, wd, xstack, dstack, cstack,
+    gtok_ref, gprob_ref, gg_ref, gu_ref, gd_ref,
+    wg, wu, wd, xstack, dstack, cstack, x_ref, d_ref, h_ref, dg_ref, du_ref, turned,
     xsend, dsend, bsend, xrecv, drecv, brecv, psend, precv, pmat,
     wsem, xs, xr, ds, dr, bs, br, ps, pr,
 ):
@@ -56,11 +56,32 @@
             barrier, inc=1, device_id=where((me + i) % n), device_id_type=MESH
         )
 
+    older = lax.broadcasted_iota(jnp.int32, (tok, tok), 0)
+    newer = lax.broadcasted_iota(jnp.int32, (tok, tok), 1)
+    eye = older == newer
+
+    def column(row):
+        return jnp.sum(jnp.where(eye, row, 0.0), axis=1, keepdims=True)
+
+    eid_row = jnp.where(keep_ref[...] == 1, ids_ref[...], -1).astype(jnp.float32)
+    eid = column(eid_row)
+    same = eid == eid_row
+    slot_row = jnp.sum(
+        jnp.where(same & (older < newer), 1.0, 0.0), axis=0, keepdims=True
+    )
+    slot = jnp.sum(jnp.where(same & (newer < older), 1.0, 0.0), axis=1, keepdims=True)
+
+    def target(e, j):
+        return jnp.where(e >= 0.0, e * block + j * PIECES, -1.0 * block).astype(jnp.int32)
+
+    tgt_row, tgt = target(eid_row, slot_row), target(eid, slot)
+    prob = column(prob_ref[...])
+
     for k in range(PIECES):
         cols = slice(k * piece, (k + 1) * piece)
         at = slice(k * tok, (k + 1) * tok)
         xstack[at, :] = tok_ref[:, cols]
-        dstack[at, :] = (prob_ref[...] * cot_ref[:, cols].astype(jnp.float32)).astype(
+        dstack[at, :] = (prob * cot_ref[:, cols].astype(jnp.float32)).astype(
             jnp.bfloat16
         )
 
@@ -82,7 +103,7 @@
         at = lax.broadcasted_iota(jnp.int32, (GROUP * block, tok), 0) + base * block
         route = jnp.concatenate(
             [
-                (at == tgt_row_ref[...] + k).astype(jnp.float32).astype(jnp.bfloat16)
+                (at == tgt_row + k).astype(jnp.float32).astype(jnp.bfloat16)
                 for k in range(PIECES)
             ],
             axis=1,
@@ -142,8 +163,8 @@
         at = pl.ds(pl.multiple_of(i * rows, rows), rows)
         take(xsend, xrecv, xs, xr, base, x_ref, at)
         x = x_ref[at, :]
-        g = f32dot(x, wg[...])
-        u = f32dot(x, wu[...])
+        g = f32dot(x, wg[...], NT)
+        u = f32dot(x, wu[...], NT)
         sig = 1.0 / (1.0 + jnp.exp(-g))
         silu = g * sig
         h = (silu * u).astype(jnp.bfloat16)
@@ -155,11 +176,11 @@
         du = (dh * silu).astype(jnp.bfloat16)
         dg_ref[at, :] = dg
         du_ref[at, :] = du
-        dx = (f32dot(dg, wg[...], NT) + f32dot(du, wu[...], NT)).astype(jnp.bfloat16)
+        dx = (f32dot(dg, wg[...]) + f32dot(du, wu[...])).astype(jnp.bfloat16)
         for k in range(PIECES):
             cstack[k * rows:(k + 1) * rows, :] = dx[:, k * piece:(k + 1) * piece]
         bsend[pl.ds(base, GROUP)] = (
-            f32dot(perm_ref[...], cstack[...], TN)
+            f32dot(unperm_ref[...], cstack[...])
             .astype(jnp.bfloat16)
             .reshape(GROUP, block, piece)
         )
@@ -183,6 +204,16 @@
         def _():
             brecv[me] = bsend[me]
             precv[me] = psend[me]
+
+    for left, right_ref, out_ref in (
+        (dg_ref, x_ref, gg_ref), (du_ref, x_ref, gu_ref), (h_ref, d_ref, gd_ref)
+    ):
+        turned[...] = left[...].T
+
+        @pl.loop(0, PIECES)
+        def _(k):
+            cols = pl.ds(pl.multiple_of(k * piece, piece), piece)
+            out_ref[:, cols] = f32dot(turned[...], right_ref[:, cols]).astype(jnp.bfloat16)
 
     @pl.loop(0, n)
     def _(s):
@@ -196,17 +227,18 @@
     back = brecv[...].reshape(n * block, piece)
     at = lax.broadcasted_iota(jnp.int32, (tok, n * block), 1)
     for k in range(PIECES):
-        route = (at == tgt_ref[...] + k).astype(jnp.float32).astype(jnp.bfloat16)
+        route = (at == tgt + k).astype(jnp.float32).astype(jnp.bfloat16)
         gtok_ref[:, k * piece:(k + 1) * piece] = f32dot(route, back).astype(jnp.bfloat16)
-    pick = (lax.broadcasted_iota(jnp.int32, (tok, n), 1) == eid_ref[...]).astype(jnp.float32)
+    pick = (lax.broadcasted_iota(jnp.int32, (tok, n), 1) == eid.astype(jnp.int32)).astype(jnp.float32)
     found = lax.dot_general(
         pick, pmat[...], (((1,), (0,)), ((), ())),
         precision=lax.Precision.HIGHEST, preferred_element_type=jnp.float32,
     )
     found = jnp.where(
-        lax.broadcasted_iota(jnp.int32, (tok, 128), 1) == slot_ref[...], found, 0.0
-    )
-    gprob_ref[...] = jnp.sum(found, axis=1, keepdims=True) / prob_ref[...]
+        lax.broadcasted_iota(jnp.int32, (tok, 128), 1) == slot.astype(jnp.int32), found, 0.0
+    )
+    found = jnp.sum(found, axis=1, keepdims=True)
+    gprob_ref[...] = jnp.sum(jnp.where(eye, found, 0.0), axis=0, keepdims=True) / prob_ref[...]
 
     @pl.loop(0, n)
     def _(d):
@@ -216,13 +248,6 @@
             copy(dsend, drecv, ds, dr, d).wait_send()
             copy(bsend, brecv, bs, br, d).wait_send()
             copy(psend, precv, ps, pr, d).wait_send()
-
-
-def weight_kernel(x_ref, d_ref, h_ref, dg_ref, du_ref, gg_ref, gu_ref, gd_ref):
-    x = x_ref[...]
-    gg_ref[0] = f32dot(x, dg_ref[...], TN).astype(jnp.bfloat16)
-    gu_ref[0] = f32dot(x, du_ref[...], TN).astype(jnp.bfloat16)
-    gd_ref[0] = f32dot(h_ref[...], d_ref[...], TN).astype(jnp.bfloat16)
 
 
 def on_device(tokens, cotangent, gate_prob, expert_ids, keep_mask, w_gate, w_up, w_down):
@@ -235,14 +260,6 @@
     block = cap * PIECES
     rows = GROUP * cap
 
-    ids = expert_ids[:, 0]
-    kept = keep_mask == 1
-    order = jnp.arange(tok, dtype=jnp.int32)
-    earlier = (ids[:, None] == ids[None, :]) & kept[None, :] & (order[None, :] < order[:, None])
-    slot = jnp.sum(earlier.astype(jnp.int32), axis=1)
-    target = jnp.where(kept, ids * block + slot * PIECES, -block)
-    owner = jnp.where(kept, ids, -1)
-
     r = np.arange(GROUP * block)
     source, rest = r // block, r % block
     perm = np.zeros((GROUP * block, GROUP * block), np.float32)
@@ -253,61 +270,42 @@
     bf16, f32 = jnp.bfloat16, jnp.float32
     buf = pltpu.VMEM((n, block, piece), bf16)
     small = pltpu.VMEM((n, 1, 128), f32)
-    gtok, gprob, x, d, h, dg, du = pl.pallas_call(
+    weight = pltpu.VMEM((hidden, width), bf16)
+    inner = pltpu.VMEM((n * cap, hidden), bf16)
+    gtok, gprob, ggate, gup, gdown = pl.pallas_call(
         functools.partial(exchange_kernel, n, n_narrow, cap),
         out_shape=(
             jax.ShapeDtypeStruct((tok, width), bf16),
-            jax.ShapeDtypeStruct((tok, 1), f32),
-            jax.ShapeDtypeStruct((n * cap, width), bf16),
-            jax.ShapeDtypeStruct((n * cap, width), bf16),
-            jax.ShapeDtypeStruct((n * cap, hidden), bf16),
-            jax.ShapeDtypeStruct((n * cap, hidden), bf16),
-            jax.ShapeDtypeStruct((n * cap, hidden), bf16),
+            jax.ShapeDtypeStruct((1, tok), f32),
+            jax.ShapeDtypeStruct((hidden, width), bf16),
+            jax.ShapeDtypeStruct((hidden, width), bf16),
+            jax.ShapeDtypeStruct((hidden, width), bf16),
         ),
-        in_specs=[vmem] * 8 + [hbm] * 3,
-        out_specs=(vmem,) * 7,
+        in_specs=[vmem] * 7 + [hbm] * 3,
+        out_specs=(vmem,) * 5,
         scratch_shapes=[
-            pltpu.VMEM((width, hidden), bf16),
-            pltpu.VMEM((width, hidden), bf16),
-            pltpu.VMEM((hidden, width), bf16),
+            weight, weight, weight,
             pltpu.VMEM((PIECES * tok, piece), bf16),
             pltpu.VMEM((PIECES * tok, piece), bf16),
             pltpu.VMEM((GROUP * block, piece), bf16),
+            pltpu.VMEM((n * cap, width), bf16),
+            pltpu.VMEM((n * cap, width), bf16),
+            inner, inner, inner,
+            pltpu.VMEM((hidden, n * cap), bf16),
             buf, buf, buf, buf, buf, buf, small, small,
             pltpu.VMEM((n, 128), f32),
             pltpu.SemaphoreType.DMA((3,)),
         ] + [pltpu.SemaphoreType.DMA((n,))] * 8,
         compiler_params=pltpu.CompilerParams(
-            collective_id=0, has_side_effects=True, vmem_limit_bytes=48 * 1024 * 1024
+            collective_id=0, has_side_effects=True, vmem_limit_bytes=42 * 1024 * 1024
         ),
         name="exchange",
     )(
-        tokens, cotangent, gate_prob[:, None], target[None, :], target[:, None],
-        owner[:, None], slot[:, None], jnp.asarray(perm, bf16),
-        w_gate[0], w_up[0], w_down[0],
-    )
-
-    tile = 256
-    full = pl.BlockSpec((n * cap, hidden), lambda i: (0, 0))
-    part = pl.BlockSpec((n * cap, tile), lambda i: (0, i))
-    ggate, gup, gdown = pl.pallas_call(
-        weight_kernel,
-        grid=(width // tile,),
-        out_shape=(
-            jax.ShapeDtypeStruct((1, width, hidden), bf16),
-            jax.ShapeDtypeStruct((1, width, hidden), bf16),
-            jax.ShapeDtypeStruct((1, hidden, width), bf16),
-        ),
-        in_specs=[part, part, full, full, full],
-        out_specs=(
-            pl.BlockSpec((1, tile, hidden), lambda i: (0, i, 0)),
-            pl.BlockSpec((1, tile, hidden), lambda i: (0, i, 0)),
-            pl.BlockSpec((1, hidden, tile), lambda i: (0, 0, i)),
-        ),
-        compiler_params=pltpu.CompilerParams(vmem_limit_bytes=32 * 1024 * 1024),
-        name="weights",
-    )(x, d, h, dg, du)
-    return gtok, gprob[:, 0], ggate, gup, gdown
+        tokens, cotangent, gate_prob[None, :], expert_ids.reshape(1, tok), keep_mask[None, :],
+        jnp.asarray(perm, bf16), jnp.asarray(perm.T, bf16),
+        w_gate[0].T, w_up[0].T, w_down[0],
+    )
+    return gtok, gprob[0], ggate.T[None], gup.T[None], gdown[None]
 
 
 def solution(mesh):

time: 103 us -> 76.2 us (0.74)
  local copies, waits for them, and re-layouts: 29.3 us -> 12 us
  Pallas kernels: 69.1 us -> 63.2 us
  other arithmetic: 2.87 us -> 0 us
    unnamed x31 -> x19, local copies, waits for them, and re-layouts: 28.2 us -> 12 us
    pallas_call x1 -> x0, Pallas kernels: 5.53 us -> none  [on_device(): pl.pallas_call(weight_kernel, grid=(width // tile,), out_shape=(jax.Shape...]
    broadcast_in_dim x4 -> x0, local copies, waits for them, and re-layouts: 1.1 us -> none  [the longest x1 0.76 us: on_device(): gate_prob[:, None]]
where the time goes in v2:
time: 76.2 us; the launch traced here: 75.9 us
  Pallas kernels  63.2 us (83%)
  local copies, waits for them, and re-layouts  12 us (16%)
    pallas_call x1, Pallas kernels, on_device(): pl.pallas_call(functools.partial(exchange_kernel, n, n_narrow, cap), out_...  63.2 us
    unnamed x19, local copies, waits for them, and re-layouts  12 us

profile of v2, /device:TPU:0, one launch (start us, length us, event | category | flops | bytes accessed | tf_op | source)
XLA Modules:
  0.0 75.9 jit_solution(9971707045686047645)
XLA Ops:
  0.6 0.0 copy-start
  0.6 1.0 %copy-done = bf16[128,2048]{1,0:T(8,128)(2,1)S(1)} copy-done((bf16[128,2048]{1,0:T(8,128)(2,1)S(1)}, bf16[128,2048]{1,0:T(8,128)(2,1)}, u32[]{:S(2)}) %copy-start) | copy-done | bytes 524312
  1.7 0.0 copy-start.1
  1.7 1.0 %copy-done.1 = bf16[128,2048]{1,0:T(8,128)(2,1)S(1)} copy-done((bf16[128,2048]{1,0:T(8,128)(2,1)S(1)}, bf16[128,2048]{1,0:T(8,128)(2,1)}, u32[]{:S(2)}) %copy-start.1) | copy-done | bytes 524312
  2.7 0.0 copy-start.2
  2.7 1.0 %copy-done.2 = bf16[384,384]{1,0:T(8,128)(2,1)S(1)} copy-done((bf16[384,384]{1,0:T(8,128)(2,1)S(1)}, bf16[384,384]{1,0:T(8,128)(2,1)}, u32[]{:S(2)}) %copy-start.2) | copy-done | bytes 294936
  3.7 0.0 copy-start.3
  3.7 1.0 %copy-done.3 = bf16[384,384]{1,0:T(8,128)(2,1)S(1)} copy-done((bf16[384,384]{1,0:T(8,128)(2,1)S(1)}, bf16[384,384]{1,0:T(8,128)(2,1)}, u32[]{:S(2)}) %copy-start.3) | copy-done | bytes 294936
  4.6 0.0 copy-start.4
  4.6 0.7 copy-done.4
  5.3 0.0 copy-start.5
  5.3 0.7 copy-done.5
  6.0 0.0 copy-start.6
  6.0 0.7 copy-done.6
  6.6 63.2 %exchange.1 = (bf16[128,2048]{1,0:T(8,128)(2,1)S(1)}, f32[1,128]{1,0:T(1,128)S(1)}, bf16[704,2048]{1,0:T(8,128)(2,1)S(1)}, bf16[704,2048]{1,0:T(8,128)(2,1)S(1)}, bf16[704,2048]{1,0:T(8,128)(2,1)S(1)}) custom-call(bf16[128,2048]{1,0:T(8,128)(2,1)S(1)} %copy-done, bf16[128,2048]{1,0:T(8,128)(2,1)S(1)} %copy-done.1, f32[1,128]{1,0:T(1,128)S(1)} %bitcast.21, ...), custom_call_target="tpu_custom_call" | custom-call | tf_op jit(solution)/shard_map/exchange/pallas_call | solution.py:275
  69.8 0.8 %copy.20 = bf16[128,2048]{1,0:T(8,128)(2,1)} copy(bf16[128,2048]{1,0:T(8,128)(2,1)S(1)} %get-tuple-element.20) | data formatting | bytes 1048576
  70.6 0.5 copy.21
  71.2 1.6 %copy.22 = bf16[1,2048,704]{1,2,0:T(8,128)(2,1)} copy(bf16[1,2048,704]{1,2,0:T(8,128)(2,1)S(1)} %bitcast.20) | data formatting | bytes 5767168
  72.7 1.6 %copy.23 = bf16[1,2048,704]{1,2,0:T(8,128)(2,1)} copy(bf16[1,2048,704]{1,2,0:T(8,128)(2,1)S(1)} %bitcast.19) | data formatting | bytes 5767168
  74.3 1.6 %copy.24 = bf16[1,704,2048]{2,1,0:T(8,128)(2,1)} copy(bf16[1,704,2048]{2,1,0:T(8,128)(2,1)S(1)} %bitcast.18) | data formatting | bytes 5767168
Async XLA Ops:
  0.6 1.0 %copy-start = (bf16[128,2048]{1,0:T(8,128)(2,1)S(1)}, bf16[128,2048]{1,0:T(8,128)(2,1)}, u32[]{:S(2)}) copy-start(bf16[128,2048]{1,0:T(8,128)(2,1)} %tok_ref.1) | copy-start | bytes 1572868
  1.7 1.0 %copy-start.1 = (bf16[128,2048]{1,0:T(8,128)(2,1)S(1)}, bf16[128,2048]{1,0:T(8,128)(2,1)}, u32[]{:S(2)}) copy-start(bf16[128,2048]{1,0:T(8,128)(2,1)} %cot_ref.1) | copy-start | bytes 1572868
  2.7 1.0 %copy-start.2 = (bf16[384,384]{1,0:T(8,128)(2,1)S(1)}, bf16[384,384]{1,0:T(8,128)(2,1)}, u32[]{:S(2)}) copy-start(bf16[384,384]{1,0:T(8,128)(2,1)} %constant.5.clone.unperm_ref) | copy-start | bytes 884740
  3.7 1.0 %copy-start.3 = (bf16[384,384]{1,0:T(8,128)(2,1)S(1)}, bf16[384,384]{1,0:T(8,128)(2,1)}, u32[]{:S(2)}) copy-start(bf16[384,384]{1,0:T(8,128)(2,1)} %constant.4.clone.perm_ref) | copy-start | bytes 884740
  4.6 0.7 copy-start.4
  5.3 0.7 copy-start.5
  6.0 0.7 copy-start.6

commit v3 on v2

--- a/solution.py
+++ b/solution.py
@@ -2,7 +2,6 @@
 
 import jax
 import jax.numpy as jnp
-import numpy as np
 from jax import lax
 from jax.experimental import pallas as pl
 from jax.experimental.pallas import tpu as pltpu
@@ -21,10 +20,11 @@
 
 def exchange_kernel(
     n, n_narrow, cap,
-    tok_ref, cot_ref, prob_ref, ids_ref, keep_ref, perm_ref, unperm_ref,
+    tok_ref, cot_ref, row_ref,
     wg_hbm, wu_hbm, wd_hbm,
     gtok_ref, gprob_ref, gg_ref, gu_ref, gd_ref,
     wg, wu, wd, xstack, dstack, cstack, x_ref, d_ref, h_ref, dg_ref, du_ref, turned,
+    perm_ref, unperm_ref, gsum,
     xsend, dsend, bsend, xrecv, drecv, brecv, psend, precv, pmat,
     wsem, xs, xr, ds, dr, bs, br, ps, pr,
 ):
@@ -63,7 +63,7 @@
     def column(row):
         return jnp.sum(jnp.where(eye, row, 0.0), axis=1, keepdims=True)
 
-    eid_row = jnp.where(keep_ref[...] == 1, ids_ref[...], -1).astype(jnp.float32)
+    prob_row, eid_row = row_ref[0:1, :], row_ref[1:2, :]
     eid = column(eid_row)
     same = eid == eid_row
     slot_row = jnp.sum(
@@ -75,7 +75,7 @@
         return jnp.where(e >= 0.0, e * block + j * PIECES, -1.0 * block).astype(jnp.int32)
 
     tgt_row, tgt = target(eid_row, slot_row), target(eid, slot)
-    prob = column(prob_ref[...])
+    prob = column(prob_row)
 
     for k in range(PIECES):
         cols = slice(k * piece, (k + 1) * piece)
@@ -134,6 +134,13 @@
     @pl.loop(1, groups)
     def _(i):
         fill(i, False)
+
+    size = GROUP * block
+    one = lax.broadcasted_iota(jnp.int32, (size, size), 0)
+    other = lax.broadcasted_iota(jnp.int32, (size, size), 1)
+    for a, b, out in ((one, other, perm_ref), (other, one, unperm_ref)):
+        hit = b == (a % rows) * PIECES + a // rows
+        out[...] = hit.astype(jnp.float32).astype(jnp.bfloat16)
 
     for load in loads:
         load.wait()
@@ -215,20 +222,30 @@
             cols = pl.ds(pl.multiple_of(k * piece, piece), piece)
             out_ref[:, cols] = f32dot(turned[...], right_ref[:, cols]).astype(jnp.bfloat16)
 
-    @pl.loop(0, n)
-    def _(s):
-        @pl.when(s != me)
-        def _():
-            arrival(bsend, brecv, bs, br, s).wait_recv()
-            arrival(psend, precv, ps, pr, s).wait_recv()
-
-        pmat[pl.ds(s, 1), :] = precv[s]
-
-    back = brecv[...].reshape(n * block, piece)
-    at = lax.broadcasted_iota(jnp.int32, (tok, n * block), 1)
-    for k in range(PIECES):
-        route = (at == tgt + k).astype(jnp.float32).astype(jnp.bfloat16)
-        gtok_ref[:, k * piece:(k + 1) * piece] = f32dot(route, back).astype(jnp.bfloat16)
+    gsum[...] = jnp.zeros_like(gsum)
+
+    @pl.loop(0, groups)
+    def _(i):
+        base = ((mine - i + groups) % groups) * GROUP
+
+        @pl.loop(0, GROUP)
+        def _(q):
+            s = base + q
+
+            @pl.when(s != me)
+            def _():
+                arrival(bsend, brecv, bs, br, s).wait_recv()
+                arrival(psend, precv, ps, pr, s).wait_recv()
+
+            pmat[pl.ds(s, 1), :] = precv[s]
+
+        back = brecv[pl.ds(base, GROUP)].reshape(size, piece)
+        at = lax.broadcasted_iota(jnp.int32, (tok, size), 1) + base * block
+        for k in range(PIECES):
+            route = (at == tgt + k).astype(jnp.float32).astype(jnp.bfloat16)
+            gsum[:, k * piece:(k + 1) * piece] += f32dot(route, back)
+
+    gtok_ref[...] = gsum[...].astype(jnp.bfloat16)
     pick = (lax.broadcasted_iota(jnp.int32, (tok, n), 1) == eid.astype(jnp.int32)).astype(jnp.float32)
     found = lax.dot_general(
         pick, pmat[...], (((1,), (0,)), ((), ())),
@@ -238,7 +255,7 @@
         lax.broadcasted_iota(jnp.int32, (tok, 128), 1) == slot.astype(jnp.int32), found, 0.0
     )
     found = jnp.sum(found, axis=1, keepdims=True)
-    gprob_ref[...] = jnp.sum(jnp.where(eye, found, 0.0), axis=0, keepdims=True) / prob_ref[...]
+    gprob_ref[...] = jnp.sum(jnp.where(eye, found, 0.0), axis=0, keepdims=True) / prob_row
 
     @pl.loop(0, n)
     def _(d):
@@ -250,6 +267,18 @@
             copy(psend, precv, ps, pr, d).wait_send()
 
 
+def store_kernel(*refs):
+    sem = refs[-1]
+    count = len(refs) // 2
+    moves = [
+        pltpu.make_async_copy(refs[i], refs[count + i], sem.at[i]) for i in range(count)
+    ]
+    for move in moves:
+        move.start()
+    for move in moves:
+        move.wait()
+
+
 def on_device(tokens, cotangent, gate_prob, expert_ids, keep_mask, w_gate, w_up, w_down):
     tok, width = tokens.shape
     hidden = w_gate.shape[2]
@@ -258,12 +287,9 @@
     cap = max(2, 5 * tok // (4 * n) + 1)
     piece = width // PIECES
     block = cap * PIECES
-    rows = GROUP * cap
-
-    r = np.arange(GROUP * block)
-    source, rest = r // block, r % block
-    perm = np.zeros((GROUP * block, GROUP * block), np.float32)
-    perm[(rest % PIECES) * rows + source * cap + rest // PIECES, r] = 1.0
+
+    owner = jnp.where(keep_mask == 1, expert_ids.reshape(tok), -1).astype(jnp.float32)
+    row = jnp.stack([gate_prob, owner])
 
     vmem = pl.BlockSpec(memory_space=pltpu.VMEM)
     hbm = pl.BlockSpec(memory_space=pl.ANY)
@@ -272,7 +298,7 @@
     small = pltpu.VMEM((n, 1, 128), f32)
     weight = pltpu.VMEM((hidden, width), bf16)
     inner = pltpu.VMEM((n * cap, hidden), bf16)
-    gtok, gprob, ggate, gup, gdown = pl.pallas_call(
+    parts = pl.pallas_call(
         functools.partial(exchange_kernel, n, n_narrow, cap),
         out_shape=(
             jax.ShapeDtypeStruct((tok, width), bf16),
@@ -281,7 +307,7 @@
             jax.ShapeDtypeStruct((hidden, width), bf16),
             jax.ShapeDtypeStruct((hidden, width), bf16),
         ),
-        in_specs=[vmem] * 7 + [hbm] * 3,
+        in_specs=[vmem] * 3 + [hbm] * 3,
         out_specs=(vmem,) * 5,
         scratch_shapes=[
             weight, weight, weight,
@@ -292,6 +318,9 @@
             pltpu.VMEM((n * cap, width), bf16),
             inner, inner, inner,
             pltpu.VMEM((hidden, n * cap), bf16),
+            pltpu.VMEM((GROUP * block, GROUP * block), bf16),
+            pltpu.VMEM((GROUP * block, GROUP * block), bf16),
+            pltpu.VMEM((tok, width), f32),
             buf, buf, buf, buf, buf, buf, small, small,
             pltpu.VMEM((n, 128), f32),
             pltpu.SemaphoreType.DMA((3,)),
@@ -301,10 +330,18 @@
         ),
         name="exchange",
     )(
-        tokens, cotangent, gate_prob[None, :], expert_ids.reshape(1, tok), keep_mask[None, :],
-        jnp.asarray(perm, bf16), jnp.asarray(perm.T, bf16),
+        tokens, cotangent, row,
         w_gate[0].T, w_up[0].T, w_down[0],
     )
+    gtok, gprob, ggate, gup, gdown = pl.pallas_call(
+        store_kernel,
+        out_shape=[jax.ShapeDtypeStruct(a.shape, a.dtype) for a in parts],
+        in_specs=[hbm] * len(parts),
+        out_specs=[hbm] * len(parts),
+        scratch_shapes=[pltpu.SemaphoreType.DMA((len(parts),))],
+        compiler_params=pltpu.CompilerParams(vmem_limit_bytes=1024 * 1024),
+        name="store",
+    )(*parts)
     return gtok, gprob[0], ggate.T[None], gup.T[None], gdown[None]
 
 

time: 76.2 us -> 70.7 us (0.928)
  local copies, waits for them, and re-layouts: 12 us -> 2.08 us
  Pallas kernels: 63.2 us -> 66.4 us
  other arithmetic: 0 us -> 1.34 us
    unnamed x19 -> x4, local copies, waits for them, and re-layouts: 12 us -> 2.08 us
    pallas_call x0 -> x1, Pallas kernels: none -> 3.7 us  [on_device(): pl.pallas_call(store_kernel, out_shape=[jax.ShapeDtypeStruct(a.shape, a.d...]
    another operation x0 -> x2, other arithmetic: none -> 1.34 us  [on_device(): row = jnp.stack([gate_prob, owner])]
where the time goes in v3:
time: 70.7 us; the launch traced here: 70.5 us
  Pallas kernels  66.4 us (94%)
  local copies, waits for them, and re-layouts  2.08 us (3%)
  other arithmetic  1.34 us (2%)
    pallas_call x1, Pallas kernels, on_device(): pl.pallas_call(functools.partial(exchange_kernel, n, n_narrow, cap), out_...  62.7 us
    pallas_call x1, Pallas kernels, on_device(): pl.pallas_call(store_kernel, out_shape=[jax.ShapeDtypeStruct(a.shape, a.d...  3.7 us
    unnamed x4, local copies, waits for them, and re-layouts  2.08 us

profile of v3, /device:TPU:0, one launch (start us, length us, event | category | flops | bytes accessed | tf_op | source)
XLA Modules:
  0.0 70.5 jit_solution(2498862875608618529)
XLA Ops:
  0.6 0.7 fusion.1
  1.3 0.7 pad_maximum_fusion.row_ref
  2.0 0.0 copy-start
  2.0 1.0 %copy-done = bf16[128,2048]{1,0:T(8,128)(2,1)S(1)} copy-done((bf16[128,2048]{1,0:T(8,128)(2,1)S(1)}, bf16[128,2048]{1,0:T(8,128)(2,1)}, u32[]{:S(2)}) %copy-start) | copy-done | bytes 524312
  3.0 0.0 copy-start.1
  3.0 1.0 %copy-done.1 = bf16[128,2048]{1,0:T(8,128)(2,1)S(1)} copy-done((bf16[128,2048]{1,0:T(8,128)(2,1)S(1)}, bf16[128,2048]{1,0:T(8,128)(2,1)}, u32[]{:S(2)}) %copy-start.1) | copy-done | bytes 524312
  4.1 62.7 %exchange.1 = (bf16[128,2048]{1,0:T(8,128)(2,1)S(1)}, f32[1,128]{1,0:T(1,128)S(1)}, bf16[704,2048]{1,0:T(8,128)(2,1)S(1)}, bf16[704,2048]{1,0:T(8,128)(2,1)S(1)}, bf16[704,2048]{1,0:T(8,128)(2,1)S(1)}) custom-call(bf16[128,2048]{1,0:T(8,128)(2,1)S(1)} %copy-done, bf16[128,2048]{1,0:T(8,128)(2,1)S(1)} %copy-done.1, f32[2,128]{1,0:T(2,128)S(1)} %pad_maximum_fusion.row_ref, ...), custom_call_target="tpu_custom_call" | custom-call | tf_op jit(solution)/shard_map/exchange/pallas_call | solution.py:301
  66.8 3.7 %store.1 = (bf16[128,2048]{1,0:T(8,128)(2,1)}, f32[1,128]{1,0:T(1,128)}, bf16[704,2048]{1,0:T(8,128)(2,1)}, bf16[704,2048]{1,0:T(8,128)(2,1)}, bf16[704,2048]{1,0:T(8,128)(2,1)}) custom-call(bf16[128,2048]{1,0:T(8,128)(2,1)S(1)} %get-tuple-element.15.refs_0_, f32[1,128]{1,0:T(1,128)S(1)} %get-tuple-element.16.refs_1_, ...), custom_call_target="tpu_custom_call" | custom-call | tf_op jit(solution)/shard_map/store/pallas_call | solution.py:336
Async XLA Ops:
  2.0 1.0 %copy-start = (bf16[128,2048]{1,0:T(8,128)(2,1)S(1)}, bf16[128,2048]{1,0:T(8,128)(2,1)}, u32[]{:S(2)}) copy-start(bf16[128,2048]{1,0:T(8,128)(2,1)} %tok_ref.1) | copy-start | bytes 1572868
  3.0 1.0 %copy-start.1 = (bf16[128,2048]{1,0:T(8,128)(2,1)S(1)}, bf16[128,2048]{1,0:T(8,128)(2,1)}, u32[]{:S(2)}) copy-start(bf16[128,2048]{1,0:T(8,128)(2,1)} %cot_ref.1) | copy-start | bytes 1572868

commit v4 on v3

--- a/solution.py
+++ b/solution.py
@@ -108,16 +108,14 @@
             ],
             axis=1,
         )
-        xsend[pl.ds(base, GROUP)] = (
-            f32dot(route, xstack[...]).astype(jnp.bfloat16).reshape(GROUP, block, piece)
-        )
-        dsend[pl.ds(base, GROUP)] = (
-            f32dot(route, dstack[...]).astype(jnp.bfloat16).reshape(GROUP, block, piece)
-        )
-        if first:
-            pl.semaphore_wait(barrier, n - 1)
-
-        for send, recv, ss, rs in ((xsend, xrecv, xs, xr), (dsend, drecv, ds, dr)):
+        for send, recv, ss, rs, stack in (
+            (xsend, xrecv, xs, xr, xstack), (dsend, drecv, ds, dr, dstack)
+        ):
+            send[pl.ds(base, GROUP)] = (
+                f32dot(route, stack[...]).astype(jnp.bfloat16).reshape(GROUP, block, piece)
+            )
+            if first and send is xsend:
+                pl.semaphore_wait(barrier, n - 1)
 
             @pl.loop(0, GROUP)
             def _(q):

time: 70.7 us -> 70.7 us (level)
  no operation moved by 1% of the time
where the time goes in v4:
time: 70.7 us; the launch traced here: 70.5 us
  Pallas kernels  66.4 us (94%)
  local copies, waits for them, and re-layouts  2.08 us (3%)
  other arithmetic  1.34 us (2%)
    pallas_call x1, Pallas kernels, on_device(): pl.pallas_call(functools.partial(exchange_kernel, n, n_narrow, cap), out_...  62.7 us
    pallas_call x1, Pallas kernels, on_device(): pl.pallas_call(store_kernel, out_shape=[jax.ShapeDtypeStruct(a.shape, a.d...  3.7 us
    unnamed x4, local copies, waits for them, and re-layouts  2.08 us

profile of v4, /device:TPU:0, one launch (start us, length us, event | category | flops | bytes accessed | tf_op | source)
XLA Modules:
  0.0 70.5 jit_solution(16407315064846431223)
XLA Ops:
  0.6 0.7 fusion.1
  1.3 0.7 pad_maximum_fusion.row_ref
  2.0 0.0 copy-start
  2.0 1.0 %copy-done = bf16[128,2048]{1,0:T(8,128)(2,1)S(1)} copy-done((bf16[128,2048]{1,0:T(8,128)(2,1)S(1)}, bf16[128,2048]{1,0:T(8,128)(2,1)}, u32[]{:S(2)}) %copy-start) | copy-done | bytes 524312
  3.0 0.0 copy-start.1
  3.0 1.0 %copy-done.1 = bf16[128,2048]{1,0:T(8,128)(2,1)S(1)} copy-done((bf16[128,2048]{1,0:T(8,128)(2,1)S(1)}, bf16[128,2048]{1,0:T(8,128)(2,1)}, u32[]{:S(2)}) %copy-start.1) | copy-done | bytes 524312
  4.1 62.7 %exchange.1 = (bf16[128,2048]{1,0:T(8,128)(2,1)S(1)}, f32[1,128]{1,0:T(1,128)S(1)}, bf16[704,2048]{1,0:T(8,128)(2,1)S(1)}, bf16[704,2048]{1,0:T(8,128)(2,1)S(1)}, bf16[704,2048]{1,0:T(8,128)(2,1)S(1)}) custom-call(bf16[128,2048]{1,0:T(8,128)(2,1)S(1)} %copy-done, bf16[128,2048]{1,0:T(8,128)(2,1)S(1)} %copy-done.1, f32[2,128]{1,0:T(2,128)S(1)} %pad_maximum_fusion.row_ref, ...), custom_call_target="tpu_custom_call" | custom-call | tf_op jit(solution)/shard_map/exchange/pallas_call | solution.py:299
  66.8 3.7 %store.1 = (bf16[128,2048]{1,0:T(8,128)(2,1)}, f32[1,128]{1,0:T(1,128)}, bf16[704,2048]{1,0:T(8,128)(2,1)}, bf16[704,2048]{1,0:T(8,128)(2,1)}, bf16[704,2048]{1,0:T(8,128)(2,1)}) custom-call(bf16[128,2048]{1,0:T(8,128)(2,1)S(1)} %get-tuple-element.15.refs_0_, f32[1,128]{1,0:T(1,128)S(1)} %get-tuple-element.16.refs_1_, ...), custom_call_target="tpu_custom_call" | custom-call | tf_op jit(solution)/shard_map/store/pallas_call | solution.py:334
Async XLA Ops:
  2.0 1.0 %copy-start = (bf16[128,2048]{1,0:T(8,128)(2,1)S(1)}, bf16[128,2048]{1,0:T(8,128)(2,1)}, u32[]{:S(2)}) copy-start(bf16[128,2048]{1,0:T(8,128)(2,1)} %tok_ref.1) | copy-start | bytes 1572868
  3.0 1.0 %copy-start.1 = (bf16[128,2048]{1,0:T(8,128)(2,1)S(1)}, bf16[128,2048]{1,0:T(8,128)(2,1)}, u32[]{:S(2)}) copy-start(bf16[128,2048]{1,0:T(8,128)(2,1)} %cot_ref.1) | copy-start | bytes 1572868
